TPU v7x, 128 devices: a whole 4x4x4 slice. The times are simulated.
128 devices in a mesh: layer: 4 (over y), grid: 32 (over x, z, core).
Axes of the slice: x: 4, y: 4, z: 4, core: 2. Of those that a mesh axis runs over, the one named last changes fastest.
Arguments:
- leaf_inverse: float32 [4, 32, 4, 128, 128], P('layer', 'grid'), may hold values from -1 to 2
- leaf_coupling: float32 [4, 32, 4, 128, 128], P('layer', 'grid'), may hold values from -0.5 to 0.5
- leaf_rhs: float32 [4, 32, 4, 128, 128], P('layer', 'grid'), may hold values from -6 to 6
- mid_inverse: float32 [4, 32, 2, 128, 128], P('layer', 'grid'), may hold values from -1 to 2
- mid_coupling: float32 [4, 32, 2, 128, 128], P('layer', 'grid'), may hold values from -0.375 to 0.375
- mid_rhs: float32 [4, 32, 2, 128, 128], P('layer', 'grid'), may hold values from -6 to 6
- mid_top: float32 [4, 32, 2, 4096, 128], P('layer', 'grid'), may hold values from -0.0546875 to 0.0546875
- root_inverse: float32 [4, 32, 128, 128], P('layer', 'grid'), may hold values from -1 to 2
- root_top: float32 [4, 32, 4096, 128], P('layer', 'grid'), may hold values from -0.0546875 to 0.0546875
- root_rhs: float32 [4, 32, 128, 128], P('layer', 'grid'), may hold values from -6 to 6
- top_inverse: float32 [32, 128, 128], P('grid'), may hold values from -1 to 2
- top_factor: float32 [32, 128, 4096], P('grid'), may hold values from -0.25 to 0.25
- top_rhs: float32 [32, 128, 128], P('grid'), may hold values from -6 to 6
- top_pattern: int32 [32, 32], P('grid'), may hold values from 0 to 1, as said below
Outputs:
- leaf_solution: float32 [4, 32, 4, 128, 128], P('layer', 'grid')
- mid_solution: float32 [4, 32, 2, 128, 128], P('layer', 'grid')
- root_solution: float32 [4, 32, 128, 128], P('layer', 'grid')
- top_solution: float32 [32, 128, 128], P('grid')
Inputs may be any that keep to these rules, and one draw needn't show every extreme that they name: `top_pattern`: entries (i, j) with j // 4 >= i // 4 are not read; entry (i, 0) is 1 for every i >= 4.
All inputs are finite; a program needn't handle non-finite values.
Results may differ from a plain program's by a relative error of at most 0.00011.
Values sent between devices are 32-bit elements; how exact they have to be, the bound alone decides.
No kernel may reach another device: no remote copies, remote signals or barrier semaphores. Data moves between devices by JAX's collectives and lax.ppermute only.
A program may use at most 64 MiB of HBM per device.

v0:
```python
import jax
import jax.numpy as jnp
from jax import lax
from jax.sharding import PartitionSpec as P

SPAN = 4


def product(spec, left, right):
    return jnp.einsum(
        spec, left, right, precision=lax.Precision.HIGHEST, preferred_element_type=jnp.float32
    )


def transposed(left, right):
    return lax.dot_general(
        left,
        right,
        (((0,), (0,)), ((), ())),
        precision=lax.Precision.HIGHEST,
        preferred_element_type=jnp.float32,
    )


def pack_slot(value, slot, span):
    picks = (jnp.arange(span) == slot)[:, None, None]
    return jnp.where(picks, value[None], jnp.zeros((), jnp.float32))


def local(
    leaf_inverse,
    leaf_coupling,
    leaf_rhs,
    mid_inverse,
    mid_coupling,
    mid_rhs,
    mid_top,
    root_inverse,
    root_top,
    root_rhs,
    top_inverse,
    top_factor,
    top_rhs,
    top_pattern,
):
    block_width = leaf_inverse.shape[-1]
    columns = leaf_rhs.shape[-1]
    blocks_top = lax.axis_size("grid")
    position = lax.axis_index("grid")
    span = SPAN
    group_count = blocks_top // span
    own_group = position // span
    leaf_inv = leaf_inverse[0, 0]
    leaf_links = leaf_coupling[0, 0]
    forward_leaf = product("pab,pbr->par", leaf_inv, leaf_rhs[0, 0])
    pulled = (
        product("pab,pbr->par", leaf_links, forward_leaf)
        .reshape(-1, 2, block_width, columns)
        .sum(axis=1)
    )
    forward_mid = product("mab,mbr->mar", mid_inverse[0, 0], mid_rhs[0, 0] - pulled)
    root_input = root_rhs[0, 0] - product("mab,mbr->ar", mid_coupling[0, 0], forward_mid)
    forward_root = product("ab,br->ar", root_inverse[0, 0], root_input)
    root_panel = root_top[0, 0]
    mid_panel = mid_top[0, 0]
    root_rows = root_panel
    mid_rows = mid_panel
    summed = product("kb,br->kr", root_rows, forward_root) + product(
        "mkb,mbr->kr", mid_rows, forward_mid
    )
    partial_sums = lax.psum_scatter(
        summed.reshape(1 * lax.axis_size("grid"), block_width, columns),
        "grid",
        scatter_dimension=0,
        tiled=True,
    )
    reduced = lax.psum(partial_sums, "layer")
    residual = top_rhs[0] - reduced[0]
    top_inv = top_inverse[0]
    factor_row = top_factor[0]
    pattern_row = top_pattern[0]

    def weights_of(group):
        stored = lax.dynamic_slice_in_dim(pattern_row, group * span, span)
        return jnp.where(group < own_group, stored, 0).astype(jnp.float32)

    def panel_of(group):
        return lax.dynamic_slice_in_dim(
            factor_row, group * span * block_width, span * block_width, 1
        )

    def forward_step(group, carried):
        residual, solved_own = carried
        candidate = jnp.dot(
            top_inv, residual, precision=lax.Precision.HIGHEST, preferred_element_type=jnp.float32
        )
        slot = position - group * span
        solved = lax.psum(pack_slot(candidate, slot, span), "grid")
        scaled = (weights_of(group)[:, None, None] * solved).reshape(span * block_width, columns)
        update = jnp.dot(
            panel_of(group),
            scaled,
            precision=lax.Precision.HIGHEST,
            preferred_element_type=jnp.float32,
        )
        residual = residual - update
        solved_own = jnp.where(own_group == group, candidate, solved_own)
        return (residual, solved_own)

    residual, forward_top = lax.fori_loop(
        0, group_count, forward_step, (residual, jnp.zeros_like(residual))
    )

    def contribution(group, back_own):
        terms = transposed(panel_of(group), back_own).reshape(span, block_width, columns)
        return weights_of(group)[:, None, None] * terms

    def settle(group, pulled_group, back_own):
        slot = jnp.clip(position - group * span, 0, span - 1)
        pulled_top = lax.dynamic_index_in_dim(pulled_group, slot, 0, keepdims=False)
        candidate = transposed(top_inv, forward_top - pulled_top)
        return jnp.where(own_group == group, candidate, back_own)

    def back_step(sweep_step, back_own):
        group = group_count - 1 - sweep_step
        pulled_group = lax.psum(contribution(group, back_own), "grid")
        return settle(group, pulled_group, back_own)

    back_own = lax.fori_loop(0, group_count, back_step, jnp.zeros_like(forward_top))
    shard_piece = lax.all_gather(back_own[None], "grid", axis=0, tiled=True)
    amount = shard_piece.shape[0]
    flat_rows = shard_piece.reshape(amount * block_width, columns)
    root_rows = root_panel
    mid_rows = mid_panel
    root_pull = transposed(root_rows, flat_rows)
    mid_pull = product("mkb,kr->mbr", mid_rows, flat_rows)
    back_root = product("ba,br->ar", root_inverse[0, 0], forward_root - root_pull)
    back_mid = product(
        "mba,mbr->mar",
        mid_inverse[0, 0],
        forward_mid - product("mab,ar->mbr", mid_coupling[0, 0], back_root) - mid_pull,
    )
    parent = jnp.repeat(back_mid, 2, axis=0)
    back_leaf = product(
        "pba,pbr->par", leaf_inv, forward_leaf - product("pab,par->pbr", leaf_links, parent)
    )
    return (back_leaf[None, None], back_mid[None, None], back_root[None, None], back_own[None])


def solution(mesh):
    placed = (
        P("layer", "grid", None, None, None),
        P("layer", "grid", None, None, None),
        P("layer", "grid", None, None, None),
        P("layer", "grid", None, None, None),
        P("layer", "grid", None, None, None),
        P("layer", "grid", None, None, None),
        P("layer", "grid", None, None, None),
        P("layer", "grid", None, None),
        P("layer", "grid", None, None),
        P("layer", "grid", None, None),
        P("grid", None, None),
        P("grid", None, None),
        P("grid", None, None),
        P("grid", None),
    )
    return jax.shard_map(
        local,
        mesh=mesh,
        in_specs=placed,
        out_specs=(
            P("layer", "grid", None, None, None),
            P("layer", "grid", None, None, None),
            P("layer", "grid", None, None),
            P("grid", None, None),
        ),
        check_vma=False,
    )
```

profile of v0, /device:TPU:1, one launch (start us, length us, event | category | flops | bytes accessed | tf_op | source)
XLA Modules:
  0.0 1938.6 jit_solution(1425876203916425412)
XLA Ops:
  12.7 6.5 convolution_bitcast_fusion.1
  26.2 80.7 %reduce-scatter.2.cloned.1.call-done = f32[1,128,128]{2,1,0:T(8,128)} async-done(((f32[32,128,128]{2,1,0:T(8,128)}), f32[1,128,128]{2,1,0:T(8,128)}) %reduce-scatter.2.cloned.1.call-update) | async-done | bytes 65552 | tf_op jit(solution)/shard_map/reduce_scatter | solution.py:71
  106.9 41.9 %all-reduce.4.cloned.1.call-done = f32[1,128,128]{2,1,0:T(8,128)} async-done(((f32[1,128,128]{2,1,0:T(8,128)}), f32[1,128,128]{2,1,0:T(8,128)}) %all-reduce.4.cloned.1.call-update) | async-done | bytes 65552 | tf_op jit(solution)/shard_map/psum | solution.py:77
  149.7 868.9 %while.34 = (s32[]{:T(128)}, f32[128,128]{1,0:T(8,128)S(1)}, f32[128,128]{1,0:T(8,128)S(1)}, f32[128,4096]{1,0:T(8,128)}, s32[]{:T(128)}, /*index=5*/s32[32]{0:T...) while((s32[]{:T(128)}, f32[128,128]{1,0:T(8,128)S(1)}, ...), condition=%wide.region_5.6_spmd.clone, body=%wide.region_3.5_spmd.clone.sunk | while | flops 126074896 | bytes 3408247 | solution.py:110
  150.9 107.7 %all-reduce.6.cloned.1.call-done = f32[4,128,128]{2,1,0:T(8,128)} async-done(((f32[4,128,128]{2,1,0:T(8,128)}), f32[4,128,128]{2,1,0:T(8,128)}) %all-reduce.6.cloned.1.call-update) | async-done | bytes 262160 | tf_op jit(solution)/shard_map/while/body/eval_jaxpr/psum | solution.py:98
  262.2 104.5 %all-reduce.6.cloned.1.call-done = f32[4,128,128]{2,1,0:T(8,128)} async-done(((f32[4,128,128]{2,1,0:T(8,128)}), f32[4,128,128]{2,1,0:T(8,128)}) %all-reduce.6.cloned.1.call-update) | async-done | bytes 262160 | tf_op jit(solution)/shard_map/while/body/eval_jaxpr/psum | solution.py:98
  370.3 104.5 %all-reduce.6.cloned.1.call-done = f32[4,128,128]{2,1,0:T(8,128)} async-done(((f32[4,128,128]{2,1,0:T(8,128)}), f32[4,128,128]{2,1,0:T(8,128)}) %all-reduce.6.cloned.1.call-update) | async-done | bytes 262160 | tf_op jit(solution)/shard_map/while/body/eval_jaxpr/psum | solution.py:98
  478.4 104.5 %all-reduce.6.cloned.1.call-done = f32[4,128,128]{2,1,0:T(8,128)} async-done(((f32[4,128,128]{2,1,0:T(8,128)}), f32[4,128,128]{2,1,0:T(8,128)}) %all-reduce.6.cloned.1.call-update) | async-done | bytes 262160 | tf_op jit(solution)/shard_map/while/body/eval_jaxpr/psum | solution.py:98
  586.5 104.8 %all-reduce.6.cloned.1.call-done = f32[4,128,128]{2,1,0:T(8,128)} async-done(((f32[4,128,128]{2,1,0:T(8,128)}), f32[4,128,128]{2,1,0:T(8,128)}) %all-reduce.6.cloned.1.call-update) | async-done | bytes 262160 | tf_op jit(solution)/shard_map/while/body/eval_jaxpr/psum | solution.py:98
  694.9 104.8 %all-reduce.6.cloned.1.call-done = f32[4,128,128]{2,1,0:T(8,128)} async-done(((f32[4,128,128]{2,1,0:T(8,128)}), f32[4,128,128]{2,1,0:T(8,128)}) %all-reduce.6.cloned.1.call-update) | async-done | bytes 262160 | tf_op jit(solution)/shard_map/while/body/eval_jaxpr/psum | solution.py:98
  803.3 104.8 %all-reduce.6.cloned.1.call-done = f32[4,128,128]{2,1,0:T(8,128)} async-done(((f32[4,128,128]{2,1,0:T(8,128)}), f32[4,128,128]{2,1,0:T(8,128)}) %all-reduce.6.cloned.1.call-update) | async-done | bytes 262160 | tf_op jit(solution)/shard_map/while/body/eval_jaxpr/psum | solution.py:98
  911.7 104.5 %all-reduce.6.cloned.1.call-done = f32[4,128,128]{2,1,0:T(8,128)} async-done(((f32[4,128,128]{2,1,0:T(8,128)}), f32[4,128,128]{2,1,0:T(8,128)}) %all-reduce.6.cloned.1.call-update) | async-done | bytes 262160 | tf_op jit(solution)/shard_map/while/body/eval_jaxpr/psum | solution.py:98
  1018.6 852.6 %while.35 = (s32[]{:T(128)}, f32[128,128]{0,1:T(8,128)S(1)}, s32[]{:T(128)}, s32[32]{0:T(128)S(1)}, f32[128,4096]{1,0:T(8,128)}, /*index=5*/s32[]{:T(128)}, f32[...) while((s32[]{:T(128)}, f32[128,128]{0,1:T(8,128)S(1)}, ...), condition=%wide.region_8.9_spmd.clone, body=%wide.region_6.8_spmd.clone.sunk | while | flops 126025744 | bytes 3015076 | solution.py:129
  1021.2 103.1 %all-reduce.8.cloned.1.call-done = f32[4,128,128]{2,1,0:T(8,128)} async-done(((f32[4,128,128]{2,1,0:T(8,128)}), f32[4,128,128]{2,1,0:T(8,128)}) %all-reduce.8.cloned.1.call-update) | async-done | bytes 262160 | tf_op jit(solution)/shard_map/while/body/eval_jaxpr/psum | solution.py:126
  1128.0 102.8 %all-reduce.8.cloned.1.call-done = f32[4,128,128]{2,1,0:T(8,128)} async-done(((f32[4,128,128]{2,1,0:T(8,128)}), f32[4,128,128]{2,1,0:T(8,128)}) %all-reduce.8.cloned.1.call-update) | async-done | bytes 262160 | tf_op jit(solution)/shard_map/while/body/eval_jaxpr/psum | solution.py:126
  1234.5 103.1 %all-reduce.8.cloned.1.call-done = f32[4,128,128]{2,1,0:T(8,128)} async-done(((f32[4,128,128]{2,1,0:T(8,128)}), f32[4,128,128]{2,1,0:T(8,128)}) %all-reduce.8.cloned.1.call-update) | async-done | bytes 262160 | tf_op jit(solution)/shard_map/while/body/eval_jaxpr/psum | solution.py:126
  1341.3 102.8 %all-reduce.8.cloned.1.call-done = f32[4,128,128]{2,1,0:T(8,128)} async-done(((f32[4,128,128]{2,1,0:T(8,128)}), f32[4,128,128]{2,1,0:T(8,128)}) %all-reduce.8.cloned.1.call-update) | async-done | bytes 262160 | tf_op jit(solution)/shard_map/while/body/eval_jaxpr/psum | solution.py:126
  1447.8 102.8 %all-reduce.8.cloned.1.call-done = f32[4,128,128]{2,1,0:T(8,128)} async-done(((f32[4,128,128]{2,1,0:T(8,128)}), f32[4,128,128]{2,1,0:T(8,128)}) %all-reduce.8.cloned.1.call-update) | async-done | bytes 262160 | tf_op jit(solution)/shard_map/while/body/eval_jaxpr/psum | solution.py:126
  1554.3 102.8 %all-reduce.8.cloned.1.call-done = f32[4,128,128]{2,1,0:T(8,128)} async-done(((f32[4,128,128]{2,1,0:T(8,128)}), f32[4,128,128]{2,1,0:T(8,128)}) %all-reduce.8.cloned.1.call-update) | async-done | bytes 262160 | tf_op jit(solution)/shard_map/while/body/eval_jaxpr/psum | solution.py:126
  1660.8 102.8 %all-reduce.8.cloned.1.call-done = f32[4,128,128]{2,1,0:T(8,128)} async-done(((f32[4,128,128]{2,1,0:T(8,128)}), f32[4,128,128]{2,1,0:T(8,128)}) %all-reduce.8.cloned.1.call-update) | async-done | bytes 262160 | tf_op jit(solution)/shard_map/while/body/eval_jaxpr/psum | solution.py:126
  1767.3 102.8 %all-reduce.8.cloned.1.call-done = f32[4,128,128]{2,1,0:T(8,128)} async-done(((f32[4,128,128]{2,1,0:T(8,128)}), f32[4,128,128]{2,1,0:T(8,128)}) %all-reduce.8.cloned.1.call-update) | async-done | bytes 262160 | tf_op jit(solution)/shard_map/while/body/eval_jaxpr/psum | solution.py:126
  1873.6 46.3 %all-gather.3.cloned.1.call-done = f32[4096,128]{0,1:T(8,128)} async-done(((f32[128,128]{0,1:T(8,128)}), f32[4096,128]{0,1:T(8,128)}) %all-gather.3.cloned.1.call-update) | async-done | bytes 2097168 | tf_op jit(solution)/shard_map/all_gather | solution.py:130
  1919.9 3.9 fusion.34
  1924.3 3.8 fusion.28
  (164 shorter events, 77.0 us)
Async XLA Ops:
  7.2 12.7 copy-start
  7.2 99.7 %reduce-scatter.2.cloned.1.call-start = ((), (), s32[]{:S(2)}) async-start(), calls=%async_computation.1 | async-start | bytes 2162688 | tf_op jit(solution)/shard_map/reduce_scatter | solution.py:71
  12.7 6.8 copy-start.8
  26.1 122.7 %copy-start.9 = (f32[1,128,128]{2,1,0:T(8,128)S(1)}, f32[1,128,128]{2,1,0:T(8,128)}, u32[]{:S(2)}) copy-start(f32[1,128,128]{2,1,0:T(8,128)} %param.30) | copy-start | bytes 196612
  26.1 123.6 %copy-start.3 = (f32[1,128,128]{2,1,0:T(8,128)S(1)}, f32[1,128,128]{2,1,0:T(8,128)}, u32[]{:S(2)}) copy-start(f32[1,128,128]{2,1,0:T(8,128)} %param.28) | copy-start | bytes 196612
  26.1 123.6 %copy-start.11 = (s32[1,32]{1,0:T(1,128)S(1)}, s32[1,32]{1,0:T(1,128)}, u32[]{:S(2)}) copy-start(s32[1,32]{1,0:T(1,128)} %param.31) | copy-start | bytes 388
  26.2 122.7 %all-reduce.4.cloned.1.call-start = ((), (), s32[]{:S(2)}) async-start(), calls=%async_computation.2 | async-start | bytes 131072 | tf_op jit(solution)/shard_map/psum | solution.py:77
  149.7 108.9 %all-reduce.6.cloned.1.call-start = ((), (), s32[]{:S(2)}) async-start(), calls=%async_computation.4 | async-start | bytes 524288 | tf_op jit(solution)/shard_map/while/body/eval_jaxpr/psum | solution.py:98
  261.0 105.7 %all-reduce.6.cloned.1.call-start = ((), (), s32[]{:S(2)}) async-start(), calls=%async_computation.4 | async-start | bytes 524288 | tf_op jit(solution)/shard_map/while/body/eval_jaxpr/psum | solution.py:98
  369.1 105.7 %all-reduce.6.cloned.1.call-start = ((), (), s32[]{:S(2)}) async-start(), calls=%async_computation.4 | async-start | bytes 524288 | tf_op jit(solution)/shard_map/while/body/eval_jaxpr/psum | solution.py:98
  477.2 105.7 %all-reduce.6.cloned.1.call-start = ((), (), s32[]{:S(2)}) async-start(), calls=%async_computation.4 | async-start | bytes 524288 | tf_op jit(solution)/shard_map/while/body/eval_jaxpr/psum | solution.py:98
  585.3 106.0 %all-reduce.6.cloned.1.call-start = ((), (), s32[]{:S(2)}) async-start(), calls=%async_computation.4 | async-start | bytes 524288 | tf_op jit(solution)/shard_map/while/body/eval_jaxpr/psum | solution.py:98
  693.7 106.0 %all-reduce.6.cloned.1.call-start = ((), (), s32[]{:S(2)}) async-start(), calls=%async_computation.4 | async-start | bytes 524288 | tf_op jit(solution)/shard_map/while/body/eval_jaxpr/psum | solution.py:98
  802.1 106.0 %all-reduce.6.cloned.1.call-start = ((), (), s32[]{:S(2)}) async-start(), calls=%async_computation.4 | async-start | bytes 524288 | tf_op jit(solution)/shard_map/while/body/eval_jaxpr/psum | solution.py:98
  910.5 105.7 %all-reduce.6.cloned.1.call-start = ((), (), s32[]{:S(2)}) async-start(), calls=%async_computation.4 | async-start | bytes 524288 | tf_op jit(solution)/shard_map/while/body/eval_jaxpr/psum | solution.py:98
  1018.6 105.7 %all-reduce.8.cloned.1.call-start = ((), (), s32[]{:S(2)}) async-start(), calls=%async_computation.5 | async-start | bytes 524288 | tf_op jit(solution)/shard_map/while/body/eval_jaxpr/psum | solution.py:126
  1125.5 105.4 %all-reduce.8.cloned.1.call-start = ((), (), s32[]{:S(2)}) async-start(), calls=%async_computation.5 | async-start | bytes 524288 | tf_op jit(solution)/shard_map/while/body/eval_jaxpr/psum | solution.py:126
  1232.0 105.7 %all-reduce.8.cloned.1.call-start = ((), (), s32[]{:S(2)}) async-start(), calls=%async_computation.5 | async-start | bytes 524288 | tf_op jit(solution)/shard_map/while/body/eval_jaxpr/psum | solution.py:126
  1338.8 105.3 %all-reduce.8.cloned.1.call-start = ((), (), s32[]{:S(2)}) async-start(), calls=%async_computation.5 | async-start | bytes 524288 | tf_op jit(solution)/shard_map/while/body/eval_jaxpr/psum | solution.py:126
  1445.3 105.4 %all-reduce.8.cloned.1.call-start = ((), (), s32[]{:S(2)}) async-start(), calls=%async_computation.5 | async-start | bytes 524288 | tf_op jit(solution)/shard_map/while/body/eval_jaxpr/psum | solution.py:126
  1551.8 105.3 %all-reduce.8.cloned.1.call-start = ((), (), s32[]{:S(2)}) async-start(), calls=%async_computation.5 | async-start | bytes 524288 | tf_op jit(solution)/shard_map/while/body/eval_jaxpr/psum | solution.py:126
  1658.3 105.4 %all-reduce.8.cloned.1.call-start = ((), (), s32[]{:S(2)}) async-start(), calls=%async_computation.5 | async-start | bytes 524288 | tf_op jit(solution)/shard_map/while/body/eval_jaxpr/psum | solution.py:126
  1764.8 105.3 %all-reduce.8.cloned.1.call-start = ((), (), s32[]{:S(2)}) async-start(), calls=%async_computation.5 | async-start | bytes 524288 | tf_op jit(solution)/shard_map/while/body/eval_jaxpr/psum | solution.py:126
  1871.3 48.7 %all-gather.3.cloned.1.call-start = ((), (), s32[]{:S(2)}) async-start(), calls=%async_computation.3 | async-start | bytes 2162688 | tf_op jit(solution)/shard_map/all_gather | solution.py:130
  (7 other events, 27.2 us)
Sparse Core Ops, SparseCore 0:
  26.3 80.5 reduce-scatter.1
  109.2 39.6 all-reduce.3
  154.7 103.8 all-reduce.5
  265.7 100.9 all-reduce.5
  373.8 100.9 all-reduce.5
  481.9 100.9 all-reduce.5
  590.3 100.9 all-reduce.5
  698.7 100.9 all-reduce.5
  807.1 100.9 all-reduce.5
  915.2 100.9 all-reduce.5
  1023.3 100.9 all-reduce.7
  1129.8 100.9 all-reduce.7
  1236.6 100.9 all-reduce.7
  1343.1 100.9 all-reduce.7
  1449.6 100.9 all-reduce.7
  1556.1 100.9 all-reduce.7
  1662.6 100.9 all-reduce.7
  1769.1 100.9 all-reduce.7
  1875.1 44.7 all-gather.2
where the time goes:
time: 1940 us
  waiting for transfers between devices  1830 us (94%)
  matrix products  58.2 us (3%)
  other arithmetic  23.1 us (1%)
    psum x8, waiting for transfers between devices, forward_step(): solved = lax.psum(pack_slot(candidate, slot, span), 'grid')  840 us
    psum x8, waiting for transfers between devices, back_step(): pulled_group = lax.psum(contribution(group, back_own), 'grid')  823 us
    reduce_scatter x1, waiting for transfers between devices, local(): lax.psum_scatter(summed.reshape(1 * lax.axis_size('grid'), block_width, c...  80.7 us
    all_gather x1, waiting for transfers between devices, local(): shard_piece = lax.all_gather(back_own[None], 'grid', axis=0, tiled=True)  46.3 us
    psum x1, waiting for transfers between devices, local(): reduced = lax.psum(partial_sums, 'layer')  41.9 us
  transfers between devices with their start and end apart: 19, of which 19 were waited for; matrix products, arithmetic and copies ran while one was open for 0% of the time, Pallas kernels for 0%

commit v1 on v0

--- a/solution.py
+++ b/solution.py
@@ -74,7 +74,9 @@
         scatter_dimension=0,
         tiled=True,
     )
-    reduced = lax.psum(partial_sums, "layer")
+    reduced = partial_sums
+    for hop in (1, 2):
+        reduced = reduced + lax.ppermute(reduced, "layer", [(dev, dev ^ hop) for dev in range(4)])
     residual = top_rhs[0] - reduced[0]
     top_inv = top_inverse[0]
     factor_row = top_factor[0]

time: 1940 us -> 1910 us (0.985)
  waiting for transfers between devices: 1830 us -> 1800 us
    psum x1 -> x0, waiting for transfers between devices: 41.9 us -> none  [local(): reduced = lax.psum(partial_sums, 'layer')]
  transfers between devices with their start and end apart: 19 -> 20, of which waited for: 19 -> 20; matrix products, arithmetic and copies ran while one was open for 0% -> 0% of each run, Pallas kernels for 0% -> 0%
where the time goes in v1:
time: 1910 us
  waiting for transfers between devices  1800 us (94%)
  matrix products  58.2 us (3%)
  other arithmetic  23.1 us (1%)
    psum x8, waiting for transfers between devices, forward_step(): solved = lax.psum(pack_slot(candidate, slot, span), 'grid')  839 us
    psum x8, waiting for transfers between devices, back_step(): pulled_group = lax.psum(contribution(group, back_own), 'grid')  826 us
    reduce_scatter x1, waiting for transfers between devices, local(): lax.psum_scatter(summed.reshape(1 * lax.axis_size('grid'), block_width, c...  80.7 us
    all_gather x1, waiting for transfers between devices, local(): shard_piece = lax.all_gather(back_own[None], 'grid', axis=0, tiled=True)  45.9 us
  transfers between devices with their start and end apart: 20, of which 20 were waited for; matrix products, arithmetic and copies ran while one was open for 0% of the time, Pallas kernels for 0%

profile of v1, /device:TPU:1, one launch (start us, length us, event | category | flops | bytes accessed | tf_op | source)
XLA Modules:
  0.0 1906.0 jit_solution(17261903448020268999)
XLA Ops:
  12.7 6.5 convolution_bitcast_fusion.1
  19.8 3.4 fusion.14
  26.2 80.7 %reduce-scatter.2.cloned.1.call-done = f32[1,128,128]{2,1,0:T(8,128)} async-done(((f32[32,128,128]{2,1,0:T(8,128)}), f32[1,128,128]{2,1,0:T(8,128)}) %reduce-scatter.2.cloned.1.call-update) | async-done | bytes 65552 | tf_op jit(solution)/shard_map/reduce_scatter | solution.py:71
  115.9 867.7 %while.34 = (s32[]{:T(128)}, f32[128,128]{1,0:T(8,128)S(1)}, f32[128,128]{1,0:T(8,128)S(1)}, f32[128,4096]{1,0:T(8,128)}, s32[]{:T(128)}, /*index=5*/s32[32]{0:T...) while((s32[]{:T(128)}, f32[128,128]{1,0:T(8,128)S(1)}, ...), condition=%wide.region_4.5_spmd.clone, body=%wide.region_2.4_spmd.clone.sunk | while | flops 126074896 | bytes 3408247 | solution.py:112
  117.1 108.5 %all-reduce.3.cloned.1.call-done = f32[4,128,128]{2,1,0:T(8,128)} async-done(((f32[4,128,128]{2,1,0:T(8,128)}), f32[4,128,128]{2,1,0:T(8,128)}) %all-reduce.3.cloned.1.call-update) | async-done | bytes 262160 | tf_op jit(solution)/shard_map/while/body/eval_jaxpr/psum | solution.py:100
  229.2 104.5 %all-reduce.3.cloned.1.call-done = f32[4,128,128]{2,1,0:T(8,128)} async-done(((f32[4,128,128]{2,1,0:T(8,128)}), f32[4,128,128]{2,1,0:T(8,128)}) %all-reduce.3.cloned.1.call-update) | async-done | bytes 262160 | tf_op jit(solution)/shard_map/while/body/eval_jaxpr/psum | solution.py:100
  337.3 104.1 %all-reduce.3.cloned.1.call-done = f32[4,128,128]{2,1,0:T(8,128)} async-done(((f32[4,128,128]{2,1,0:T(8,128)}), f32[4,128,128]{2,1,0:T(8,128)}) %all-reduce.3.cloned.1.call-update) | async-done | bytes 262160 | tf_op jit(solution)/shard_map/while/body/eval_jaxpr/psum | solution.py:100
  445.0 104.1 %all-reduce.3.cloned.1.call-done = f32[4,128,128]{2,1,0:T(8,128)} async-done(((f32[4,128,128]{2,1,0:T(8,128)}), f32[4,128,128]{2,1,0:T(8,128)}) %all-reduce.3.cloned.1.call-update) | async-done | bytes 262160 | tf_op jit(solution)/shard_map/while/body/eval_jaxpr/psum | solution.py:100
  552.8 104.1 %all-reduce.3.cloned.1.call-done = f32[4,128,128]{2,1,0:T(8,128)} async-done(((f32[4,128,128]{2,1,0:T(8,128)}), f32[4,128,128]{2,1,0:T(8,128)}) %all-reduce.3.cloned.1.call-update) | async-done | bytes 262160 | tf_op jit(solution)/shard_map/while/body/eval_jaxpr/psum | solution.py:100
  660.6 104.5 %all-reduce.3.cloned.1.call-done = f32[4,128,128]{2,1,0:T(8,128)} async-done(((f32[4,128,128]{2,1,0:T(8,128)}), f32[4,128,128]{2,1,0:T(8,128)}) %all-reduce.3.cloned.1.call-update) | async-done | bytes 262160 | tf_op jit(solution)/shard_map/while/body/eval_jaxpr/psum | solution.py:100
  768.7 104.5 %all-reduce.3.cloned.1.call-done = f32[4,128,128]{2,1,0:T(8,128)} async-done(((f32[4,128,128]{2,1,0:T(8,128)}), f32[4,128,128]{2,1,0:T(8,128)}) %all-reduce.3.cloned.1.call-update) | async-done | bytes 262160 | tf_op jit(solution)/shard_map/while/body/eval_jaxpr/psum | solution.py:100
  876.7 104.5 %all-reduce.3.cloned.1.call-done = f32[4,128,128]{2,1,0:T(8,128)} async-done(((f32[4,128,128]{2,1,0:T(8,128)}), f32[4,128,128]{2,1,0:T(8,128)}) %all-reduce.3.cloned.1.call-update) | async-done | bytes 262160 | tf_op jit(solution)/shard_map/while/body/eval_jaxpr/psum | solution.py:100
  983.6 855.3 %while.35 = (s32[]{:T(128)}, f32[128,128]{0,1:T(8,128)S(1)}, s32[]{:T(128)}, s32[32]{0:T(128)S(1)}, f32[128,4096]{1,0:T(8,128)}, /*index=5*/s32[]{:T(128)}, f32[...) while((s32[]{:T(128)}, f32[128,128]{0,1:T(8,128)S(1)}, ...), condition=%wide.region_7.8_spmd.clone, body=%wide.region_5.7_spmd.clone.sunk | while | flops 126025744 | bytes 3015076 | solution.py:131
  986.1 103.2 %all-reduce.5.cloned.1.call-done = f32[4,128,128]{2,1,0:T(8,128)} async-done(((f32[4,128,128]{2,1,0:T(8,128)}), f32[4,128,128]{2,1,0:T(8,128)}) %all-reduce.5.cloned.1.call-update) | async-done | bytes 262160 | tf_op jit(solution)/shard_map/while/body/eval_jaxpr/psum | solution.py:128
  1093.0 103.5 %all-reduce.5.cloned.1.call-done = f32[4,128,128]{2,1,0:T(8,128)} async-done(((f32[4,128,128]{2,1,0:T(8,128)}), f32[4,128,128]{2,1,0:T(8,128)}) %all-reduce.5.cloned.1.call-update) | async-done | bytes 262160 | tf_op jit(solution)/shard_map/while/body/eval_jaxpr/psum | solution.py:128
  1200.1 103.2 %all-reduce.5.cloned.1.call-done = f32[4,128,128]{2,1,0:T(8,128)} async-done(((f32[4,128,128]{2,1,0:T(8,128)}), f32[4,128,128]{2,1,0:T(8,128)}) %all-reduce.5.cloned.1.call-update) | async-done | bytes 262160 | tf_op jit(solution)/shard_map/while/body/eval_jaxpr/psum | solution.py:128
  1306.9 103.5 %all-reduce.5.cloned.1.call-done = f32[4,128,128]{2,1,0:T(8,128)} async-done(((f32[4,128,128]{2,1,0:T(8,128)}), f32[4,128,128]{2,1,0:T(8,128)}) %all-reduce.5.cloned.1.call-update) | async-done | bytes 262160 | tf_op jit(solution)/shard_map/while/body/eval_jaxpr/psum | solution.py:128
  1414.1 103.2 %all-reduce.5.cloned.1.call-done = f32[4,128,128]{2,1,0:T(8,128)} async-done(((f32[4,128,128]{2,1,0:T(8,128)}), f32[4,128,128]{2,1,0:T(8,128)}) %all-reduce.5.cloned.1.call-update) | async-done | bytes 262160 | tf_op jit(solution)/shard_map/while/body/eval_jaxpr/psum | solution.py:128
  1520.9 103.2 %all-reduce.5.cloned.1.call-done = f32[4,128,128]{2,1,0:T(8,128)} async-done(((f32[4,128,128]{2,1,0:T(8,128)}), f32[4,128,128]{2,1,0:T(8,128)}) %all-reduce.5.cloned.1.call-update) | async-done | bytes 262160 | tf_op jit(solution)/shard_map/while/body/eval_jaxpr/psum | solution.py:128
  1627.7 103.2 %all-reduce.5.cloned.1.call-done = f32[4,128,128]{2,1,0:T(8,128)} async-done(((f32[4,128,128]{2,1,0:T(8,128)}), f32[4,128,128]{2,1,0:T(8,128)}) %all-reduce.5.cloned.1.call-update) | async-done | bytes 262160 | tf_op jit(solution)/shard_map/while/body/eval_jaxpr/psum | solution.py:128
  1734.6 103.2 %all-reduce.5.cloned.1.call-done = f32[4,128,128]{2,1,0:T(8,128)} async-done(((f32[4,128,128]{2,1,0:T(8,128)}), f32[4,128,128]{2,1,0:T(8,128)}) %all-reduce.5.cloned.1.call-update) | async-done | bytes 262160 | tf_op jit(solution)/shard_map/while/body/eval_jaxpr/psum | solution.py:128
  1841.1 45.9 %all-gather.3.cloned.1.call-done = f32[4096,128]{0,1:T(8,128)} async-done(((f32[128,128]{0,1:T(8,128)}), f32[4096,128]{0,1:T(8,128)}) %all-gather.3.cloned.1.call-update) | async-done | bytes 2097168 | tf_op jit(solution)/shard_map/all_gather | solution.py:132
  1887.0 3.9 fusion.34
  1891.4 3.8 fusion.28
  (166 shorter events, 81.5 us)
Async XLA Ops:
  7.2 12.7 copy-start
  7.2 99.7 %reduce-scatter.2.cloned.1.call-start = ((), (), s32[]{:S(2)}) async-start(), calls=%async_computation.1 | async-start | bytes 2162688 | tf_op jit(solution)/shard_map/reduce_scatter | solution.py:71
  26.1 89.7 %copy-start.10 = (f32[1,128,128]{2,1,0:T(8,128)S(1)}, f32[1,128,128]{2,1,0:T(8,128)}, u32[]{:S(2)}) copy-start(f32[1,128,128]{2,1,0:T(8,128)} %param.30) | copy-start | bytes 196612
  26.1 89.7 %copy-start.3 = (f32[1,128,128]{2,1,0:T(8,128)S(1)}, f32[1,128,128]{2,1,0:T(8,128)}, u32[]{:S(2)}) copy-start(f32[1,128,128]{2,1,0:T(8,128)} %param.28) | copy-start | bytes 196612
  26.1 89.7 %copy-start.11 = (s32[1,32]{1,0:T(1,128)S(1)}, s32[1,32]{1,0:T(1,128)}, u32[]{:S(2)}) copy-start(s32[1,32]{1,0:T(1,128)} %param.31) | copy-start | bytes 388
  106.9 3.3 collective-permute-start
  111.1 4.8 collective-permute-start.1
  115.9 109.7 %all-reduce.3.cloned.1.call-start = ((), (), s32[]{:S(2)}) async-start(), calls=%async_computation.3 | async-start | bytes 524288 | tf_op jit(solution)/shard_map/while/body/eval_jaxpr/psum | solution.py:100
  228.0 105.7 %all-reduce.3.cloned.1.call-start = ((), (), s32[]{:S(2)}) async-start(), calls=%async_computation.3 | async-start | bytes 524288 | tf_op jit(solution)/shard_map/while/body/eval_jaxpr/psum | solution.py:100
  336.1 105.3 %all-reduce.3.cloned.1.call-start = ((), (), s32[]{:S(2)}) async-start(), calls=%async_computation.3 | async-start | bytes 524288 | tf_op jit(solution)/shard_map/while/body/eval_jaxpr/psum | solution.py:100
  443.8 105.4 %all-reduce.3.cloned.1.call-start = ((), (), s32[]{:S(2)}) async-start(), calls=%async_computation.3 | async-start | bytes 524288 | tf_op jit(solution)/shard_map/while/body/eval_jaxpr/psum | solution.py:100
  551.6 105.3 %all-reduce.3.cloned.1.call-start = ((), (), s32[]{:S(2)}) async-start(), calls=%async_computation.3 | async-start | bytes 524288 | tf_op jit(solution)/shard_map/while/body/eval_jaxpr/psum | solution.py:100
  659.4 105.7 %all-reduce.3.cloned.1.call-start = ((), (), s32[]{:S(2)}) async-start(), calls=%async_computation.3 | async-start | bytes 524288 | tf_op jit(solution)/shard_map/while/body/eval_jaxpr/psum | solution.py:100
  767.5 105.7 %all-reduce.3.cloned.1.call-start = ((), (), s32[]{:S(2)}) async-start(), calls=%async_computation.3 | async-start | bytes 524288 | tf_op jit(solution)/shard_map/while/body/eval_jaxpr/psum | solution.py:100
  875.5 105.7 %all-reduce.3.cloned.1.call-start = ((), (), s32[]{:S(2)}) async-start(), calls=%async_computation.3 | async-start | bytes 524288 | tf_op jit(solution)/shard_map/while/body/eval_jaxpr/psum | solution.py:100
  983.6 105.7 %all-reduce.5.cloned.1.call-start = ((), (), s32[]{:S(2)}) async-start(), calls=%async_computation.4 | async-start | bytes 524288 | tf_op jit(solution)/shard_map/while/body/eval_jaxpr/psum | solution.py:128
  1090.5 106.0 %all-reduce.5.cloned.1.call-start = ((), (), s32[]{:S(2)}) async-start(), calls=%async_computation.4 | async-start | bytes 524288 | tf_op jit(solution)/shard_map/while/body/eval_jaxpr/psum | solution.py:128
  1197.6 105.7 %all-reduce.5.cloned.1.call-start = ((), (), s32[]{:S(2)}) async-start(), calls=%async_computation.4 | async-start | bytes 524288 | tf_op jit(solution)/shard_map/while/body/eval_jaxpr/psum | solution.py:128
  1304.4 106.0 %all-reduce.5.cloned.1.call-start = ((), (), s32[]{:S(2)}) async-start(), calls=%async_computation.4 | async-start | bytes 524288 | tf_op jit(solution)/shard_map/while/body/eval_jaxpr/psum | solution.py:128
  1411.6 105.7 %all-reduce.5.cloned.1.call-start = ((), (), s32[]{:S(2)}) async-start(), calls=%async_computation.4 | async-start | bytes 524288 | tf_op jit(solution)/shard_map/while/body/eval_jaxpr/psum | solution.py:128
  1518.4 105.7 %all-reduce.5.cloned.1.call-start = ((), (), s32[]{:S(2)}) async-start(), calls=%async_computation.4 | async-start | bytes 524288 | tf_op jit(solution)/shard_map/while/body/eval_jaxpr/psum | solution.py:128
  1625.2 105.7 %all-reduce.5.cloned.1.call-start = ((), (), s32[]{:S(2)}) async-start(), calls=%async_computation.4 | async-start | bytes 524288 | tf_op jit(solution)/shard_map/while/body/eval_jaxpr/psum | solution.py:128
  1732.1 105.7 %all-reduce.5.cloned.1.call-start = ((), (), s32[]{:S(2)}) async-start(), calls=%async_computation.4 | async-start | bytes 524288 | tf_op jit(solution)/shard_map/while/body/eval_jaxpr/psum | solution.py:128
  1838.9 48.1 %all-gather.3.cloned.1.call-start = ((), (), s32[]{:S(2)}) async-start(), calls=%async_computation.2 | async-start | bytes 2162688 | tf_op jit(solution)/shard_map/all_gather | solution.py:132
  (8 other events, 34.0 us)
Sparse Core Ops, SparseCore 0:
  26.3 80.5 reduce-scatter.1
  120.5 105.0 all-reduce.2
  232.6 100.9 all-reduce.2
  340.4 100.9 all-reduce.2
  448.2 100.9 all-reduce.2
  555.9 100.9 all-reduce.2
  664.0 100.9 all-reduce.2
  772.1 100.9 all-reduce.2
  880.2 100.9 all-reduce.2
  988.3 100.9 all-reduce.4
  1095.4 100.9 all-reduce.4
  1202.2 100.9 all-reduce.4
  1309.4 100.9 all-reduce.4
  1416.2 100.9 all-reduce.4
  1523.1 100.9 all-reduce.4
  1629.9 100.9 all-reduce.4
  1736.7 100.9 all-reduce.4
  1842.2 44.7 all-gather.2
